TPU v7x, 512 devices: a whole 4x4x16 slice. The times are simulated.
512 devices in a mesh: gx: 32 (over z, core), gy: 16 (over x, y).
Axes of the slice: x: 4, y: 4, z: 16, core: 2. Of those that a mesh axis runs over, the one named last changes fastest.
Arguments:
- adjoint: float32 [3, 8, 512, 2048], P(None, None, 'gx', 'gy'), may hold values from -12 to 12
- checkpoints: bfloat16 [1, 3, 8, 512, 2048], P(None, None, None, 'gx', 'gy'), may hold values from -3 to 3
- wall_faces: int32 [2, 64, 256], P(None, 'gx', 'gy'), may hold values 0 or 1
Outputs:
- velocity: float32 [3, 8, 512, 2048], P(None, None, 'gx', 'gy')
- pressure: float32 [8, 512, 2048], P(None, 'gx', 'gy')
Inputs may be any that keep to these rules, and one draw needn't show every extreme that they name: `wall_faces`: 1 marks a no-slip face, 0 an open one.
All inputs are finite; a program needn't handle non-finite values. No bound on the sum of `wall_faces` on one device may be relied on, other than what follows from the above.
Results may differ from a plain program's by a relative error of at most 0.0003.
Values sent between devices are 32-bit elements; how exact they have to be, the bound alone decides.
No kernel may reach another device: no remote copies, remote signals or barrier semaphores. Data moves between devices by JAX's collectives and lax.ppermute only.
A program may use at most 64 MiB of HBM per device.

v0:
```python
import jax
import jax.numpy as jnp
import numpy as np
from jax import lax
from jax.sharding import PartitionSpec as P

ITERS = 4
node_points = np.array(
    [
        -1.0,
        -0.8717401485096066,
        -0.5917001814331423,
        -0.2092992179024789,
        0.2092992179024789,
        0.5917001814331423,
        0.8717401485096066,
        1.0,
    ]
)
node_weights = np.array(
    [
        0.03571428571428571,
        0.2107042271435061,
        0.3411226924835044,
        0.4124587946587038,
        0.4124587946587038,
        0.3411226924835044,
        0.2107042271435061,
        0.03571428571428571,
    ]
)
time_step = 0.05
viscosity = 0.02
highest = lax.Precision.HIGHEST


def with_halo(value, sides, width):
    for axis, dim in sides:
        size, length = (lax.axis_size(axis), value.shape[dim])
        up = [(i, (i + 1) % size) for i in range(size)]
        down = [(j, i) for i, j in up]
        last = lax.slice_in_dim(value, length - width, length, axis=dim)
        initial = lax.slice_in_dim(value, 0, width, axis=dim)
        before = lax.ppermute(last, axis, up)
        after = lax.ppermute(initial, axis, down)
        value = jnp.concatenate([before, value, after], axis=dim)
    return value


def derivative_table(points):
    identity = np.eye(points.shape[0])
    spacing = points[:, None] - points[None, :] + identity
    barycentric = 1.0 / np.prod(spacing, axis=1)
    matrix = barycentric[None, :] / barycentric[:, None] / spacing
    matrix = matrix * (1.0 - identity)
    return matrix - identity * np.sum(matrix, axis=1)[:, None]


def along_rows(nodal, matrix):
    blocked = jnp.asarray(np.kron(np.eye(nodal.shape[2] // 8), matrix), jnp.float32)
    return jnp.einsum("xk,czky->czxy", blocked, nodal, precision=highest)


def along_columns(nodal, matrix):
    size_y = nodal.shape[3]
    block_width = 128 if size_y % 128 == 0 else size_y
    blocked = jnp.asarray(np.kron(np.eye(block_width // 8), matrix).T, jnp.float32)
    grouped = nodal.reshape(
        nodal.shape[0], nodal.shape[1], nodal.shape[2], size_y // block_width, block_width
    )
    result = jnp.einsum("czxgk,kb->czxgb", grouped, blocked, precision=highest)
    return result.reshape(nodal.shape)


def along_depth(nodal, matrix):
    return jnp.einsum("ck,akxy->acxy", jnp.asarray(matrix, jnp.float32), nodal, precision=highest)


def mass_weights(size_x, size_y):
    weights = jnp.asarray(node_weights, jnp.float32)
    across_x = jnp.tile(weights, size_x // 8)
    across_y = jnp.tile(weights, size_y // 8)
    return weights[:, None, None] * across_x[None, :, None] * across_y[None, None, :]


def edge_flags(length):
    place = jnp.arange(length) % 8
    return ((place == 0) | (place == 7)).astype(jnp.float32)


def share_counts(size_x, size_y):
    return (1.0 + edge_flags(size_x))[:, None] * (1.0 + edge_flags(size_y))[None, :]


def boundary_masks(wall_faces, size_x, size_y):
    walls = jnp.repeat(jnp.repeat(wall_faces.astype(jnp.float32), 8, axis=1), 8, axis=2)
    interior = (1.0 - edge_flags(size_x))[:, None] * (1.0 - edge_flags(size_y))[None, :]
    middle = jnp.ones((6, size_x, size_y), jnp.float32)
    velocity_mask = jnp.concatenate(
        [(interior * (1.0 - walls[0]))[None], middle, (interior * (1.0 - walls[1]))[None]], axis=0
    )
    pressure_mask = jnp.concatenate(
        [(interior * walls[0])[None], middle, (interior * walls[1])[None]], axis=0
    )
    return (velocity_mask, pressure_mask)


def sum_rows(padded):
    size_x = padded.shape[2] - 2
    place = jnp.arange(size_x) % 8
    upper = (place == 7).astype(jnp.float32)[:, None]
    lower = (place == 0).astype(jnp.float32)[:, None]
    return padded[:, :, 1:-1, :] + upper * padded[:, :, 2:, :] + lower * padded[:, :, :-2, :]


def sum_columns(padded):
    size_y = padded.shape[3] - 2
    place = jnp.arange(size_y) % 8
    upper = (place == 7).astype(jnp.float32)
    lower = (place == 0).astype(jnp.float32)
    return padded[:, :, :, 1:-1] + upper * padded[:, :, :, 2:] + lower * padded[:, :, :, :-2]


def assemble_velocity(nodal):
    padded = with_halo(nodal, (("gx", 2), ("gy", 3)), 1)
    return sum_columns(sum_rows(padded))


def assemble_pressure(nodal):
    padded = with_halo(nodal, (("gx", 2), ("gy", 3)), 1)
    return sum_columns(sum_rows(padded))


def stiffness(nodal, wmass):
    derivative = derivative_table(node_points)
    transposed = derivative.T
    return (
        along_rows(wmass * along_rows(nodal, derivative), transposed)
        + along_columns(wmass * along_columns(nodal, derivative), transposed)
        + along_depth(wmass * along_depth(nodal, derivative), transposed)
    )


def inner(former, latter, inverse_share):
    return jnp.sum(former * latter * inverse_share)


def solve_pressure(source, pressure_mask, wmass, inverse_share):
    pressure = jnp.zeros_like(source)
    resid = source
    direction = source
    norm_now = jnp.zeros((), jnp.float32)
    for round_index in range(ITERS):
        image = pressure_mask * assemble_pressure(stiffness(direction, wmass))
        if round_index == 0:
            norm_now, curve = lax.psum(
                (inner(resid, resid, inverse_share), inner(direction, image, inverse_share)),
                ("gx", "gy"),
            )
        else:
            curve = lax.psum(inner(direction, image, inverse_share), ("gx", "gy"))
        step_length = norm_now / curve
        pressure = pressure + step_length * direction
        resid = resid - step_length * image
        if round_index + 1 < ITERS:
            norm_next = lax.psum(inner(resid, resid, inverse_share), ("gx", "gy"))
            direction = resid + norm_next / norm_now * direction
            norm_now = norm_next
    return pressure


def adjoint_step(velocity, forward, velocity_mask, pressure_mask, wmass, amass, inverse_share):
    derivative = derivative_table(node_points)
    flow = forward.astype(jnp.float32)
    flow_dx = along_rows(flow, derivative)
    flow_dy = along_columns(flow, derivative)
    flow_dz = along_depth(flow, derivative)
    velocity_dx = along_rows(velocity, derivative)
    velocity_dy = along_columns(velocity, derivative)
    velocity_dz = along_depth(velocity, derivative)
    transport = flow[0:1] * velocity_dx + flow[1:2] * velocity_dy + flow[2:3] * velocity_dz
    stretch = jnp.concatenate(
        [
            jnp.sum(velocity * flow_dx, axis=0, keepdims=True),
            jnp.sum(velocity * flow_dy, axis=0, keepdims=True),
            jnp.sum(velocity * flow_dz, axis=0, keepdims=True),
        ],
        axis=0,
    )
    advect = transport - stretch
    forcing = wmass * (velocity + time_step * advect) - time_step * viscosity * stiffness(
        velocity, wmass
    )
    moved = velocity_mask * assemble_velocity(forcing) / amass
    diverge = (
        along_rows(moved[0:1], derivative)
        + along_columns(moved[1:2], derivative)
        + along_depth(moved[2:3], derivative)
    )
    source = -pressure_mask * assemble_pressure(wmass * diverge)
    pressure = solve_pressure(source, pressure_mask, wmass, inverse_share)
    slopes = jnp.concatenate(
        [
            along_rows(pressure, derivative),
            along_columns(pressure, derivative),
            along_depth(pressure, derivative),
        ],
        axis=0,
    )
    correction = assemble_velocity(wmass * slopes) / amass
    return (velocity_mask * (moved - correction), pressure)


def local(adjoint, checkpoints, wall_faces):
    size_x = adjoint.shape[2]
    size_y = adjoint.shape[3]
    wmass = mass_weights(size_x, size_y)
    counts = share_counts(size_x, size_y)
    inverse_share = 1.0 / counts
    amass = wmass * counts
    velocity_mask, pressure_mask = boundary_masks(wall_faces, size_x, size_y)
    velocity = adjoint
    velocity, pressure = adjoint_step(
        velocity, checkpoints[0], velocity_mask, pressure_mask, wmass, amass, inverse_share
    )
    return (velocity, pressure[0])


def solution(mesh):
    return jax.shard_map(
        local,
        mesh=mesh,
        in_specs=(P(None, None, "gx", "gy"), P(None, None, None, "gx", "gy"), P(None, "gx", "gy")),
        out_specs=(P(None, None, "gx", "gy"), P(None, "gx", "gy")),
        check_vma=False,
    )
```

profile of v0, /device:TPU:1, one launch (start us, length us, event | category | flops | bytes accessed | tf_op | source)
XLA Modules:
  0.0 876.8 jit_solution(5244411411854615604)
XLA Ops:
  9.0 3.0 collective-permute-start
  12.1 3.9 collective-permute-start.1
  18.9 6.7 collective-permute-start.3
  34.3 3.5 collective-permute-start.5
  40.6 7.4 collective-permute-start.7
  53.3 6.4 collective-permute-start.9
  62.6 7.4 collective-permute-start.11
  72.6 108.5 %all-reduce = (f32[]{:T(128)}, f32[]{:T(128)}) all-reduce(f32[]{:T(128)} %get-tuple-element.3, f32[]{:T(128)} %get-tuple-element.2), channel_id=1, replica_groups=mesh['gx'=32,'gy'=16] {'gx','gy'}, use_global_device_ids=true, to_apply=%region_4.5 | all-reduce | flops 2 | bytes 16 | tf_op jit(solution)/shard_map/psum | solution.py:156
  183.2 98.5 %psum.58 = f32[]{:T(128)} all-reduce(f32[]{:T(128)} %multiply_reduce_fusion.4), channel_id=1, replica_groups=mesh['gx'=32,'gy'=16] {'gx','gy'}, use_global_device_ids=true, to_apply=%region_8.9 | all-reduce | flops 1 | bytes 8 | tf_op jit(solution)/shard_map/psum | solution.py:166
  284.5 2.3 collective-permute-start.12
  292.2 6.4 collective-permute-start.15
  301.8 102.7 %psum.59 = f32[]{:T(128)} all-reduce(f32[]{:T(128)} %get-tuple-element.10), channel_id=1, replica_groups=mesh['gx'=32,'gy'=16] {'gx','gy'}, use_global_device_ids=true, to_apply=%region_10.11 | all-reduce | flops 1 | bytes 8 | tf_op jit(solution)/shard_map/psum | solution.py:161
  406.6 99.3 %psum.60 = f32[]{:T(128)} all-reduce(f32[]{:T(128)} %get-tuple-element.8), channel_id=1, replica_groups=mesh['gx'=32,'gy'=16] {'gx','gy'}, use_global_device_ids=true, to_apply=%region_12.13 | all-reduce | flops 1 | bytes 8 | tf_op jit(solution)/shard_map/psum | solution.py:166
  510.8 2.3 collective-permute-done.17
  515.6 6.3 collective-permute-start.19
  524.5 104.3 %psum.61 = f32[]{:T(128)} all-reduce(f32[]{:T(128)} %get-tuple-element.6), channel_id=1, replica_groups=mesh['gx'=32,'gy'=16] {'gx','gy'}, use_global_device_ids=true, to_apply=%region_14.15 | all-reduce | flops 1 | bytes 8 | tf_op jit(solution)/shard_map/psum | solution.py:161
  630.8 98.4 %psum.62 = f32[]{:T(128)} all-reduce(f32[]{:T(128)} %multiply_reduce_fusion), channel_id=1, replica_groups=mesh['gx'=32,'gy'=16] {'gx','gy'}, use_global_device_ids=true, to_apply=%region_16.17 | all-reduce | flops 1 | bytes 8 | tf_op jit(solution)/shard_map/psum | solution.py:166
  731.9 2.3 collective-permute-start.20
  737.4 2.5 collective-permute-start.22
  739.9 6.1 collective-permute-start.23
  749.3 102.6 %psum.63 = f32[]{:T(128)} all-reduce(f32[]{:T(128)} %fusion.73), channel_id=1, replica_groups=mesh['gx'=32,'gy'=16] {'gx','gy'}, use_global_device_ids=true, to_apply=%region_18.19 | all-reduce | flops 1 | bytes 8 | tf_op jit(solution)/shard_map/psum | solution.py:161
  854.3 2.7 collective-permute-start.24
  862.2 6.7 collective-permute-start.27
  868.9 5.4 collective-permute-done.26
  (199 shorter events, 70.1 us)
Async XLA Ops:
  9.0 7.6 collective-permute-start
  12.1 4.7 collective-permute-start.1
  17.0 10.8 %collective-permute-start.2 = (f32[3,8,18,1]{3,2,1,0:T(8,128)S(1)}, f32[3,8,18,1]{3,2,1,0:T(8,128)S(1)}, u32[]{:S(2)}, u32[]{:S(2)}) collective-permute-start(f32[3,8,18,1]{3,2,1,0:T(8,128)S(1)} %get-tuple-element.15), channel_id=1, source_target_pairs={{0,1},{1,2},{2,3},{3,4},{4,5},{5,6},{6,7},{7,8},{8,9},{9,10},{10,1... | collective-permute-start | bytes 5192 | tf_op jit(solution)/shard_map/ppermute | solution.py:44
  18.9 10.3 %collective-permute-start.3 = (f32[3,8,18,1]{3,2,1,0:T(8,128)S(1)}, f32[3,8,18,1]{3,2,1,0:T(8,128)S(1)}, u32[]{:S(2)}, u32[]{:S(2)}) collective-permute-start(f32[3,8,18,1]{3,2,1,0:T(8,128)S(1)} %get-tuple-element.16), channel_id=1, source_target_pairs={{1,0},{2,1},{3,2},{4,3},{5,4},{6,5},{7,6},{8,7},{9,8},{10,9},{11,1... | collective-permute-start | bytes 5192 | tf_op jit(solution)/shard_map/ppermute | solution.py:45
  32.4 5.9 collective-permute-start.4
  34.3 4.3 collective-permute-start.5
  38.7 9.4 %collective-permute-start.6 = (f32[1,8,18,1]{3,2,1,0:T(8,128)S(1)}, f32[1,8,18,1]{3,2,1,0:T(8,128)S(1)}, u32[]{:S(2)}, u32[]{:S(2)}) collective-permute-start(f32[1,8,18,1]{3,2,1,0:T(8,128)S(1)} %get-tuple-element.32), channel_id=1, source_target_pairs={{0,1},{1,2},{2,3},{3,4},{4,5},{5,6},{6,7},{7,8},{8,9},{9,10},{10,1... | collective-permute-start | bytes 1736 | tf_op jit(solution)/shard_map/ppermute | solution.py:44
  40.6 9.1 %collective-permute-start.7 = (f32[1,8,18,1]{3,2,1,0:T(8,128)S(1)}, f32[1,8,18,1]{3,2,1,0:T(8,128)S(1)}, u32[]{:S(2)}, u32[]{:S(2)}) collective-permute-start(f32[1,8,18,1]{3,2,1,0:T(8,128)S(1)} %get-tuple-element.33), channel_id=1, source_target_pairs={{1,0},{2,1},{3,2},{4,3},{5,4},{6,5},{7,6},{8,7},{9,8},{10,9},{11,1... | collective-permute-start | bytes 1736 | tf_op jit(solution)/shard_map/ppermute | solution.py:45
  53.3 7.1 collective-permute-start.8
  53.3 7.3 collective-permute-start.9
  60.6 9.4 %collective-permute-start.10 = (f32[1,8,18,1]{3,2,1,0:T(8,128)S(1)}, f32[1,8,18,1]{3,2,1,0:T(8,128)S(1)}, u32[]{:S(2)}, u32[]{:S(2)}) collective-permute-start(f32[1,8,18,1]{3,2,1,0:T(8,128)S(1)} %get-tuple-element.30), channel_id=1, source_target_pairs={{0,1},{1,2},{2,3},{3,4},{4,5},{5,6},{6,7},{7,8},{8,9},{9,10},{10,1... | collective-permute-start | bytes 1736 | tf_op jit(solution)/shard_map/ppermute | solution.py:44
  62.6 9.0 %collective-permute-start.11 = (f32[1,8,18,1]{3,2,1,0:T(8,128)S(1)}, f32[1,8,18,1]{3,2,1,0:T(8,128)S(1)}, u32[]{:S(2)}, u32[]{:S(2)}) collective-permute-start(f32[1,8,18,1]{3,2,1,0:T(8,128)S(1)} %get-tuple-element.31), channel_id=1, source_target_pairs={{1,0},{2,1},{3,2},{4,3},{5,4},{6,5},{7,6},{8,7},{9,8},{10,9},{11,1... | collective-permute-start | bytes 1736 | tf_op jit(solution)/shard_map/ppermute | solution.py:45
  284.5 3.1 collective-permute-start.12
  289.9 10.0 %collective-permute-start.14 = (f32[1,8,18,1]{3,2,1,0:T(8,128)S(1)}, f32[1,8,18,1]{3,2,1,0:T(8,128)S(1)}, u32[]{:S(2)}, u32[]{:S(2)}) collective-permute-start(f32[1,8,18,1]{3,2,1,0:T(8,128)S(1)} %get-tuple-element.28), channel_id=1, source_target_pairs={{0,1},{1,2},{2,3},{3,4},{4,5},{5,6},{6,7},{7,8},{8,9},{9,10},{10,1... | collective-permute-start | bytes 1736 | tf_op jit(solution)/shard_map/ppermute | solution.py:44
  292.2 8.7 collective-permute-start.15
  513.3 9.1 %collective-permute-start.18 = (f32[1,8,18,1]{3,2,1,0:T(8,128)S(1)}, f32[1,8,18,1]{3,2,1,0:T(8,128)S(1)}, u32[]{:S(2)}, u32[]{:S(2)}) collective-permute-start(f32[1,8,18,1]{3,2,1,0:T(8,128)S(1)} %get-tuple-element.26), channel_id=1, source_target_pairs={{0,1},{1,2},{2,3},{3,4},{4,5},{5,6},{6,7},{7,8},{8,9},{9,10},{10,1... | collective-permute-start | bytes 1736 | tf_op jit(solution)/shard_map/ppermute | solution.py:44
  515.6 7.9 collective-permute-start.19
  731.9 3.1 collective-permute-start.20
  737.4 10.0 %collective-permute-start.22 = (f32[1,8,18,1]{3,2,1,0:T(8,128)S(1)}, f32[1,8,18,1]{3,2,1,0:T(8,128)S(1)}, u32[]{:S(2)}, u32[]{:S(2)}) collective-permute-start(f32[1,8,18,1]{3,2,1,0:T(8,128)S(1)} %get-tuple-element.24), channel_id=1, source_target_pairs={{0,1},{1,2},{2,3},{3,4},{4,5},{5,6},{6,7},{7,8},{8,9},{9,10},{10,1... | collective-permute-start | bytes 1736 | tf_op jit(solution)/shard_map/ppermute | solution.py:44
  739.9 8.4 collective-permute-start.23
  854.3 3.5 collective-permute-start.24
  857.0 3.1 collective-permute-start.25
  860.3 14.0 %collective-permute-start.26 = (f32[3,8,18,1]{3,2,1,0:T(8,128)S(1)}, f32[3,8,18,1]{3,2,1,0:T(8,128)S(1)}, u32[]{:S(2)}, u32[]{:S(2)}) collective-permute-start(f32[3,8,18,1]{3,2,1,0:T(8,128)S(1)} %get-tuple-element.13), channel_id=1, source_target_pairs={{0,1},{1,2},{2,3},{3,4},{4,5},{5,6},{6,7},{7,8},{8,9},{9,10},{10,1... | collective-permute-start | bytes 5192 | tf_op jit(solution)/shard_map/ppermute | solution.py:44
  862.2 13.1 %collective-permute-start.27 = (f32[3,8,18,1]{3,2,1,0:T(8,128)S(1)}, f32[3,8,18,1]{3,2,1,0:T(8,128)S(1)}, u32[]{:S(2)}, u32[]{:S(2)}) collective-permute-start(f32[3,8,18,1]{3,2,1,0:T(8,128)S(1)} %get-tuple-element.14), channel_id=1, source_target_pairs={{1,0},{2,1},{3,2},{4,3},{5,4},{6,5},{7,6},{8,7},{9,8},{10,9},{11,1... | collective-permute-start | bytes 5192 | tf_op jit(solution)/shard_map/ppermute | solution.py:45
  (21 other events, 28.1 us)
where the time goes:
time: 879 us; the launch traced here: 877 us
  blocking collectives  714 us (81%)
  starting transfers between devices  89.1 us (10%)
  waiting for transfers between devices  33.5 us (4%)
  between operations  10.9 us (1%)
  other arithmetic  10 us (1%)
  matrix products  9.55 us (1%)
  local copies, waits for them, and re-layouts  9.23 us (1%)
    psum x3, blocking collectives, solve_pressure(): curve = lax.psum(inner(direction, image, inverse_share), ('gx', 'gy'))  310 us
    psum x3, blocking collectives, solve_pressure(): norm_next = lax.psum(inner(resid, resid, inverse_share), ('gx', 'gy'))  296 us
    psum x1, blocking collectives, solve_pressure(): lax.psum((inner(resid, resid, inverse_share), inner(direction, image, inv...  109 us
    ppermute x14, starting transfers between devices, with_halo(): after = lax.ppermute(initial, axis, down)  60.8 us
    ppermute x14, starting transfers between devices, with_halo(): before = lax.ppermute(last, axis, up)  28.4 us
    ppermute x14, waiting for transfers between devices, with_halo(): after = lax.ppermute(initial, axis, down)  18.2 us
  transfers between devices with their start and end apart: 28, of which 27 were waited for; matrix products, arithmetic and copies ran while one was open for 0% of the time, Pallas kernels for 0%

commit v1 on v0

--- a/solution.py
+++ b/solution.py
@@ -158,7 +158,10 @@
                 ("gx", "gy"),
             )
         else:
-            curve = lax.psum(inner(direction, image, inverse_share), ("gx", "gy"))
+            _spread_tables = lambda state, axis_key, along_axis: jax.lax.psum(
+                jax.lax.psum(state, axis_key), along_axis
+            )
+            curve = _spread_tables(inner(direction, image, inverse_share), "gx", "gy")
         step_length = norm_now / curve
         pressure = pressure + step_length * direction
         resid = resid - step_length * image

time: 879 us -> 831 us (0.945)
  blocking collectives: 714 us -> 661 us
    psum x3 -> x6, blocking collectives: 310 us -> 243 us  [the longest x3 139 us: solve_pressure(): jax.lax.psum(state, axis_key)]
    psum x3, blocking collectives: 296 us -> 309 us  [solve_pressure(): norm_next = lax.psum(inner(resid, resid, inverse_share), ('gx', 'gy'))]
where the time goes in v1:
time: 831 us; the launch traced here: 826 us
  blocking collectives  661 us (80%)
  starting transfers between devices  95.9 us (12%)
  waiting for transfers between devices  29.5 us (4%)
  between operations  10.9 us (1%)
  other arithmetic  10 us (1%)
  matrix products  9.55 us (1%)
  local copies, waits for them, and re-layouts  9.23 us (1%)
    psum x3, blocking collectives, solve_pressure(): norm_next = lax.psum(inner(resid, resid, inverse_share), ('gx', 'gy'))  309 us
    psum x3, blocking collectives, solve_pressure(): jax.lax.psum(state, axis_key)  139 us
    psum x1, blocking collectives, solve_pressure(): lax.psum((inner(resid, resid, inverse_share), inner(direction, image, inv...  109 us
    psum x3, blocking collectives, solve_pressure(): jax.lax.psum(jax.lax.psum(state, axis_key), along_axis)  104 us
    ppermute x14, starting transfers between devices, with_halo(): after = lax.ppermute(initial, axis, down)  60.9 us
    ppermute x14, starting transfers between devices, with_halo(): before = lax.ppermute(last, axis, up)  35 us
    ppermute x14, waiting for transfers between devices, with_halo(): after = lax.ppermute(initial, axis, down)  16.8 us
  transfers between devices with their start and end apart: 28, of which 27 were waited for; matrix products, arithmetic and copies ran while one was open for 0% of the time, Pallas kernels for 0%

profile of v1, /device:TPU:1, one launch (start us, length us, event | category | flops | bytes accessed | tf_op | source)
XLA Modules:
  0.0 825.8 jit_solution(8232312190961975468)
XLA Ops:
  9.0 3.0 collective-permute-start
  12.1 3.9 collective-permute-start.1
  18.9 6.7 collective-permute-start.3
  34.3 3.5 collective-permute-start.5
  40.6 7.4 collective-permute-start.7
  53.3 6.4 collective-permute-start.9
  62.6 7.4 collective-permute-start.11
  72.6 108.5 %all-reduce = (f32[]{:T(128)}, f32[]{:T(128)}) all-reduce(f32[]{:T(128)} %get-tuple-element.3, f32[]{:T(128)} %get-tuple-element.2), channel_id=1, replica_groups=mesh['gx'=32,'gy'=16] {'gx','gy'}, use_global_device_ids=true, to_apply=%region_4.5 | all-reduce | flops 2 | bytes 16 | tf_op jit(solution)/shard_map/psum | solution.py:156
  183.2 98.5 %psum.79 = f32[]{:T(128)} all-reduce(f32[]{:T(128)} %multiply_reduce_fusion.4), channel_id=1, replica_groups=mesh['gx'=32,'gy'=16] {'gx','gy'}, use_global_device_ids=true, to_apply=%region_8.9 | all-reduce | flops 1 | bytes 8 | tf_op jit(solution)/shard_map/psum | solution.py:169
  292.2 6.4 collective-permute-start.15
  301.8 46.5 %psum.80 = f32[]{:T(128)} all-reduce(f32[]{:T(128)} %get-tuple-element.10), channel_id=1, replica_groups=mesh['gx'=32,'gy'=16] {'gx'}, use_global_device_ids=true, to_apply=%region_10.11 | all-reduce | flops 1 | bytes 8 | tf_op jit(solution)/shard_map/psum | solution.py:162
  348.3 34.6 %psum.81 = f32[]{:T(128)} all-reduce(f32[]{:T(128)} %psum.80), channel_id=1, replica_groups=mesh['gx'=32,'gy'=16] {'gy'}, use_global_device_ids=true, to_apply=%region_11.12 | all-reduce | flops 1 | bytes 8 | tf_op jit(solution)/shard_map/psum | solution.py:161
  385.0 105.1 %psum.82 = f32[]{:T(128)} all-reduce(f32[]{:T(128)} %get-tuple-element.8), channel_id=1, replica_groups=mesh['gx'=32,'gy'=16] {'gx','gy'}, use_global_device_ids=true, to_apply=%region_13.14 | all-reduce | flops 1 | bytes 8 | tf_op jit(solution)/shard_map/psum | solution.py:169
  498.2 3.2 collective-permute-start.18
  501.5 5.4 collective-permute-start.19
  510.1 46.5 %psum.83 = f32[]{:T(128)} all-reduce(f32[]{:T(128)} %get-tuple-element.6), channel_id=1, replica_groups=mesh['gx'=32,'gy'=16] {'gx'}, use_global_device_ids=true, to_apply=%region_15.16 | all-reduce | flops 1 | bytes 8 | tf_op jit(solution)/shard_map/psum | solution.py:162
  556.6 34.6 %psum.84 = f32[]{:T(128)} all-reduce(f32[]{:T(128)} %psum.83), channel_id=1, replica_groups=mesh['gx'=32,'gy'=16] {'gy'}, use_global_device_ids=true, to_apply=%region_16.17 | all-reduce | flops 1 | bytes 8 | tf_op jit(solution)/shard_map/psum | solution.py:161
  593.2 105.3 %psum.85 = f32[]{:T(128)} all-reduce(f32[]{:T(128)} %multiply_reduce_fusion), channel_id=1, replica_groups=mesh['gx'=32,'gy'=16] {'gx','gy'}, use_global_device_ids=true, to_apply=%region_18.19 | all-reduce | flops 1 | bytes 8 | tf_op jit(solution)/shard_map/psum | solution.py:169
  706.6 3.2 collective-permute-start.22
  709.8 5.4 collective-permute-start.23
  718.5 46.5 %psum.86 = f32[]{:T(128)} all-reduce(f32[]{:T(128)} %fusion.73), channel_id=1, replica_groups=mesh['gx'=32,'gy'=16] {'gx'}, use_global_device_ids=true, to_apply=%region_20.21 | all-reduce | flops 1 | bytes 8 | tf_op jit(solution)/shard_map/psum | solution.py:162
  764.9 34.6 %psum.87 = f32[]{:T(128)} all-reduce(f32[]{:T(128)} %psum.86), channel_id=1, replica_groups=mesh['gx'=32,'gy'=16] {'gy'}, use_global_device_ids=true, to_apply=%region_21.22 | all-reduce | flops 1 | bytes 8 | tf_op jit(solution)/shard_map/psum | solution.py:161
  801.9 6.8 collective-permute-start.24
  814.0 6.7 collective-permute-start.27
  (202 shorter events, 78.9 us)
Async XLA Ops:
  9.0 7.6 collective-permute-start
  12.1 4.7 collective-permute-start.1
  17.0 10.8 %collective-permute-start.2 = (f32[3,8,18,1]{3,2,1,0:T(8,128)S(1)}, f32[3,8,18,1]{3,2,1,0:T(8,128)S(1)}, u32[]{:S(2)}, u32[]{:S(2)}) collective-permute-start(f32[3,8,18,1]{3,2,1,0:T(8,128)S(1)} %get-tuple-element.15), channel_id=1, source_target_pairs={{0,1},{1,2},{2,3},{3,4},{4,5},{5,6},{6,7},{7,8},{8,9},{9,10},{10,1... | collective-permute-start | bytes 5192 | tf_op jit(solution)/shard_map/ppermute | solution.py:44
  18.9 10.3 %collective-permute-start.3 = (f32[3,8,18,1]{3,2,1,0:T(8,128)S(1)}, f32[3,8,18,1]{3,2,1,0:T(8,128)S(1)}, u32[]{:S(2)}, u32[]{:S(2)}) collective-permute-start(f32[3,8,18,1]{3,2,1,0:T(8,128)S(1)} %get-tuple-element.16), channel_id=1, source_target_pairs={{1,0},{2,1},{3,2},{4,3},{5,4},{6,5},{7,6},{8,7},{9,8},{10,9},{11,1... | collective-permute-start | bytes 5192 | tf_op jit(solution)/shard_map/ppermute | solution.py:45
  32.4 5.9 collective-permute-start.4
  34.3 4.3 collective-permute-start.5
  38.7 9.4 %collective-permute-start.6 = (f32[1,8,18,1]{3,2,1,0:T(8,128)S(1)}, f32[1,8,18,1]{3,2,1,0:T(8,128)S(1)}, u32[]{:S(2)}, u32[]{:S(2)}) collective-permute-start(f32[1,8,18,1]{3,2,1,0:T(8,128)S(1)} %get-tuple-element.32), channel_id=1, source_target_pairs={{0,1},{1,2},{2,3},{3,4},{4,5},{5,6},{6,7},{7,8},{8,9},{9,10},{10,1... | collective-permute-start | bytes 1736 | tf_op jit(solution)/shard_map/ppermute | solution.py:44
  40.6 9.1 %collective-permute-start.7 = (f32[1,8,18,1]{3,2,1,0:T(8,128)S(1)}, f32[1,8,18,1]{3,2,1,0:T(8,128)S(1)}, u32[]{:S(2)}, u32[]{:S(2)}) collective-permute-start(f32[1,8,18,1]{3,2,1,0:T(8,128)S(1)} %get-tuple-element.33), channel_id=1, source_target_pairs={{1,0},{2,1},{3,2},{4,3},{5,4},{6,5},{7,6},{8,7},{9,8},{10,9},{11,1... | collective-permute-start | bytes 1736 | tf_op jit(solution)/shard_map/ppermute | solution.py:45
  53.3 7.1 collective-permute-start.8
  53.3 7.3 collective-permute-start.9
  60.6 9.4 %collective-permute-start.10 = (f32[1,8,18,1]{3,2,1,0:T(8,128)S(1)}, f32[1,8,18,1]{3,2,1,0:T(8,128)S(1)}, u32[]{:S(2)}, u32[]{:S(2)}) collective-permute-start(f32[1,8,18,1]{3,2,1,0:T(8,128)S(1)} %get-tuple-element.30), channel_id=1, source_target_pairs={{0,1},{1,2},{2,3},{3,4},{4,5},{5,6},{6,7},{7,8},{8,9},{9,10},{10,1... | collective-permute-start | bytes 1736 | tf_op jit(solution)/shard_map/ppermute | solution.py:44
  62.6 9.0 %collective-permute-start.11 = (f32[1,8,18,1]{3,2,1,0:T(8,128)S(1)}, f32[1,8,18,1]{3,2,1,0:T(8,128)S(1)}, u32[]{:S(2)}, u32[]{:S(2)}) collective-permute-start(f32[1,8,18,1]{3,2,1,0:T(8,128)S(1)} %get-tuple-element.31), channel_id=1, source_target_pairs={{1,0},{2,1},{3,2},{4,3},{5,4},{6,5},{7,6},{8,7},{9,8},{10,9},{11,1... | collective-permute-start | bytes 1736 | tf_op jit(solution)/shard_map/ppermute | solution.py:45
  284.5 3.1 collective-permute-start.12
  289.9 10.0 %collective-permute-start.14 = (f32[1,8,18,1]{3,2,1,0:T(8,128)S(1)}, f32[1,8,18,1]{3,2,1,0:T(8,128)S(1)}, u32[]{:S(2)}, u32[]{:S(2)}) collective-permute-start(f32[1,8,18,1]{3,2,1,0:T(8,128)S(1)} %get-tuple-element.28), channel_id=1, source_target_pairs={{0,1},{1,2},{2,3},{3,4},{4,5},{5,6},{6,7},{7,8},{8,9},{9,10},{10,1... | collective-permute-start | bytes 1736 | tf_op jit(solution)/shard_map/ppermute | solution.py:44
  292.2 8.7 %collective-permute-start.15 = (f32[1,8,18,1]{3,2,1,0:T(8,128)S(1)}, f32[1,8,18,1]{3,2,1,0:T(8,128)S(1)}, u32[]{:S(2)}, u32[]{:S(2)}) collective-permute-start(f32[1,8,18,1]{3,2,1,0:T(8,128)S(1)} %get-tuple-element.29), channel_id=1, source_target_pairs={{1,0},{2,1},{3,2},{4,3},{5,4},{6,5},{7,6},{8,7},{9,8},{10,9},{11,1... | collective-permute-start | bytes 1736 | tf_op jit(solution)/shard_map/ppermute | solution.py:45
  492.8 3.0 collective-permute-start.16
  498.2 10.0 %collective-permute-start.18 = (f32[1,8,18,1]{3,2,1,0:T(8,128)S(1)}, f32[1,8,18,1]{3,2,1,0:T(8,128)S(1)}, u32[]{:S(2)}, u32[]{:S(2)}) collective-permute-start(f32[1,8,18,1]{3,2,1,0:T(8,128)S(1)} %get-tuple-element.26), channel_id=1, source_target_pairs={{0,1},{1,2},{2,3},{3,4},{4,5},{5,6},{6,7},{7,8},{8,9},{9,10},{10,1... | collective-permute-start | bytes 1736 | tf_op jit(solution)/shard_map/ppermute | solution.py:44
  501.5 7.6 collective-permute-start.19
  706.6 10.0 %collective-permute-start.22 = (f32[1,8,18,1]{3,2,1,0:T(8,128)S(1)}, f32[1,8,18,1]{3,2,1,0:T(8,128)S(1)}, u32[]{:S(2)}, u32[]{:S(2)}) collective-permute-start(f32[1,8,18,1]{3,2,1,0:T(8,128)S(1)} %get-tuple-element.24), channel_id=1, source_target_pairs={{0,1},{1,2},{2,3},{3,4},{4,5},{5,6},{6,7},{7,8},{8,9},{9,10},{10,1... | collective-permute-start | bytes 1736 | tf_op jit(solution)/shard_map/ppermute | solution.py:44
  709.8 7.6 collective-permute-start.23
  801.9 9.3 %collective-permute-start.24 = (f32[3,8,1,128]{3,2,1,0:T(1,128)S(1)}, f32[3,8,1,128]{3,2,1,0:T(1,128)S(1)}, u32[]{:S(2)}, u32[]{:S(2)}) collective-permute-start(f32[3,8,1,128]{3,2,1,0:T(1,128)S(1)} %get-tuple-element.17), channel_id=1, source_target_pairs={{0,16},{16,32},{32,48},{48,64},{64,80},{80,96},{96,112},{112,128},... | collective-permute-start | bytes 36872 | tf_op jit(solution)/shard_map/ppermute | solution.py:44
  808.8 3.1 collective-permute-start.25
  812.1 10.8 %collective-permute-start.26 = (f32[3,8,18,1]{3,2,1,0:T(8,128)S(1)}, f32[3,8,18,1]{3,2,1,0:T(8,128)S(1)}, u32[]{:S(2)}, u32[]{:S(2)}) collective-permute-start(f32[3,8,18,1]{3,2,1,0:T(8,128)S(1)} %get-tuple-element.13), channel_id=1, source_target_pairs={{0,1},{1,2},{2,3},{3,4},{4,5},{5,6},{6,7},{7,8},{8,9},{9,10},{10,1... | collective-permute-start | bytes 5192 | tf_op jit(solution)/shard_map/ppermute | solution.py:44
  814.0 10.3 %collective-permute-start.27 = (f32[3,8,18,1]{3,2,1,0:T(8,128)S(1)}, f32[3,8,18,1]{3,2,1,0:T(8,128)S(1)}, u32[]{:S(2)}, u32[]{:S(2)}) collective-permute-start(f32[3,8,18,1]{3,2,1,0:T(8,128)S(1)} %get-tuple-element.14), channel_id=1, source_target_pairs={{1,0},{2,1},{3,2},{4,3},{5,4},{6,5},{7,6},{8,7},{9,8},{10,9},{11,1... | collective-permute-start | bytes 5192 | tf_op jit(solution)/shard_map/ppermute | solution.py:45
  (21 other events, 28.9 us)
